TPU v7x, 32 devices: a whole 2x2x4 slice. The times are simulated.
32 devices in a mesh: group: 1, mode: 32 (over z, y, x, core).
Axes of the slice: x: 2, y: 2, z: 4, core: 2. Of those that a mesh axis runs over, the one named last changes fastest.
Arguments:
- source_field: float32 [128, 32, 256], P(('group', 'mode')), may hold values from -650 to 650
- coeff_fields: float32 [11, 32, 256], P('group'), may hold values from 0.5 to 2
- targets: int32 [128, 16], replicated, may hold values from 0 to 31, all different within a row; in each aligned block of 4 rows (0 to 3, 4 to 7, ...) at most 2 rows name the same one
- dest_slot: int32 [128, 16], replicated, may hold values from 0 to 3
- coef_mode: int32 [128, 16], replicated, may hold values from 0 to 10
- coupling: float32 [128, 16], replicated, may hold values from -1 to 1
Outputs:
- first_image: float32 [128, 32, 256], P(('group', 'mode'))
- second_image: float32 [128, 32, 256], P(('group', 'mode'))
Inputs may be any that keep to these rules, and one draw needn't show every extreme that they name: `targets`: each row names 16 different owners; the rows j held by one device along `mode` (aligned blocks of 4 rows) name no owner more than 2 times, a bound that some block reaches.
All inputs are finite; a program needn't handle non-finite values.
Results may differ from a plain program's by a relative error of at most 0.000096.
Values sent between devices are 32-bit elements; how exact they have to be, the bound alone decides.
A program may use at most 64 MiB of HBM per device.

v0:
```python
import jax
import jax.numpy as jnp
from jax import lax
from jax.sharding import PartitionSpec as P


def laplace(fields):
    padded = jnp.pad(fields, ((0, 0), (1, 1), (1, 1)))
    return (
        4.0 * fields
        - padded[:, 2:, 1:-1]
        - padded[:, :-2, 1:-1]
        - padded[:, 1:-1, 2:]
        - padded[:, 1:-1, :-2]
    )


def local(source_field, coeff_fields, targets, dest_slot, coef_mode, coupling):
    local_modes, grid_rows, grid_cols = source_field.shape
    cell_count = grid_rows * grid_cols
    devices = lax.axis_size("mode")
    own_index = lax.axis_index("mode")
    coef_count = coeff_fields.shape[0]
    fan_out = targets.shape[1]
    entries = local_modes * fan_out
    slot_count = max(2, -(-entries // devices))
    highest = lax.Precision.HIGHEST
    flat_coeff = coeff_fields.reshape(coef_count, cell_count)
    mode_iota = jnp.arange(local_modes, dtype=jnp.int32)
    coef_iota = jnp.arange(coef_count, dtype=jnp.int32)
    owner_iota = jnp.arange(devices, dtype=jnp.int32)
    first_row = own_index * local_modes
    own_targets = lax.dynamic_slice_in_dim(targets, first_row, local_modes, 0).reshape(entries)
    own_coef = lax.dynamic_slice_in_dim(coef_mode, first_row, local_modes, 0).reshape(entries)
    own_value = lax.dynamic_slice_in_dim(coupling, first_row, local_modes, 0).reshape(entries)

    def local_products(fields):
        stencil = laplace(fields).reshape(local_modes, cell_count)
        coef_hot = (own_coef[:, None] == coef_iota[None, :]).astype(jnp.float32)
        picked = jnp.dot(coef_hot, flat_coeff, precision=highest)
        stencil_rows = jnp.repeat(stencil, fan_out, axis=0)
        return own_value[:, None] * stencil_rows * picked

    def apply_galerkin(fields):
        products = local_products(fields)
        owner_hot = (own_targets[:, None] == owner_iota[None, :]).astype(jnp.int32)
        slot_rank = jnp.sum((jnp.cumsum(owner_hot, axis=0) - owner_hot) * owner_hot, axis=1)
        slot_place = own_targets * slot_count + slot_rank
        packing = (
            jnp.arange(devices * slot_count, dtype=jnp.int32)[:, None] == slot_place[None, :]
        ).astype(jnp.float32)
        outgoing = jnp.dot(packing, products, precision=highest).reshape(
            devices, slot_count, cell_count
        )
        incoming = lax.all_to_all(outgoing, "mode", split_axis=0, concat_axis=0, tiled=True)
        all_targets = targets.reshape(devices, entries)
        all_dest = dest_slot.reshape(devices, entries)
        all_hot = (all_targets[..., None] == owner_iota).astype(jnp.int32)
        all_rank = jnp.sum((jnp.cumsum(all_hot, axis=1) - all_hot) * all_hot, axis=2)
        owned_here = (all_targets == own_index).astype(jnp.float32)
        dest_hot = (all_dest[..., None] == mode_iota).astype(jnp.float32) * owned_here[..., None]
        rank_hot = (all_rank[..., None] == jnp.arange(slot_count, dtype=jnp.int32)).astype(
            jnp.float32
        )
        collect = jnp.einsum("sem,sec->msc", dest_hot, rank_hot, precision=highest)
        collect = collect.reshape(local_modes, devices * slot_count)
        result = jnp.dot(
            collect, incoming.reshape(devices * slot_count, cell_count), precision=highest
        )
        return result.reshape(local_modes, grid_rows, grid_cols)

    energy = lax.psum(jnp.sum(source_field * source_field), "mode")
    field_scale = jnp.sqrt(energy / (targets.shape[0] * cell_count) + 1e-06)
    start_field = source_field / field_scale
    first_image = apply_galerkin(start_field)
    second_image = apply_galerkin(first_image)
    return (first_image, second_image)


def solution(mesh):
    in_specs = (P(("group", "mode"), None, None), P("group", None, None), P(), P(), P(), P())
    out_specs = (P(("group", "mode"), None, None), P(("group", "mode"), None, None))
    return jax.shard_map(local, mesh=mesh, in_specs=in_specs, out_specs=out_specs, check_vma=False)
```

profile of v0, /device:TPU:0, one launch (start us, length us, event | category | flops | bytes accessed | tf_op | source)
XLA Modules:
  0.0 178.6 jit_solution(16794800739392688284)
XLA Ops:
  0.7 0.8 constant_dynamic-slice_fusion.1
  2.4 1.6 multiply_reduce_fusion
  4.0 1.0 pad.9
  5.0 0.3 copy.50
  5.3 42.3 %psum.7 = f32[]{:T(128)} all-reduce(f32[]{:T(128)} %multiply_reduce_fusion), channel_id=1, replica_groups=mesh['group'=1,'mode'=32] {'mode'}, use_global_device_ids=true, to_apply=%region_5.6 | all-reduce | flops 1 | bytes 8 | tf_op jit(solution)/shard_map/psum | solution.py:72
  48.6 1.1 fusion.7
  49.8 2.6 %fusion.26 = f32[64,8192]{1,0:T(8,128)} fusion(f32[64,8192]{1,0:T(8,128)S(1)} %get-tuple-element.8, s32[64]{0:T(128)S(1)} %multiply_add_fusion), kind=kOutput, calls=%fused_computation.44 | convolution fusion | flops 402657280 | bytes 4194560 | tf_op jit(solution)/shard_map/dot_general | solution.py:52
  52.4 3.5 %reshape.69 = f32[32,2,8192]{2,1,0:T(2,128)} reshape(f32[64,8192]{1,0:T(8,128)} %fusion.26) | data formatting | bytes 4194304 | tf_op jit(solution)/shard_map/reshape | solution.py:52
  55.8 4.7 %all-to-all-start = ((f32[32,2,8192]{2,1,0:T(2,128)}), f32[32,2,8192]{2,1,0:T(2,128)}, u32[]{:S(2)}, u32[]{:S(2)}) async-start(f32[32,2,8192]{2,1,0:T(2,128)} %reshape.69), calls=%async_computation | async-start | bytes 4194304 | tf_op jit(solution)/shard_map/all_to_all | solution.py:55
  60.8 1.7 select_reduce_fusion
  62.8 0.2 fusion.21
  63.1 46.3 %all-to-all-done = f32[32,2,8192]{2,1,0:T(2,128)} async-done(((f32[32,2,8192]{2,1,0:T(2,128)}), f32[32,2,8192]{2,1,0:T(2,128)}, u32[]{:S(2)}, u32[]{:S(2)}) %all-to-all-start) | async-done | bytes 2097184 | tf_op jit(solution)/shard_map/all_to_all | solution.py:55
  109.4 3.7 %reshape.70 = f32[64,8192]{1,0:T(8,128)} reshape(f32[32,2,8192]{2,1,0:T(2,128)} %all-to-all-done) | data formatting | bytes 4194304 | tf_op jit(solution)/shard_map/reshape | solution.py:68
  113.1 2.7 %fusion.3 = f32[4,32,256]{2,0,1:T(4,128)S(1)} fusion(f32[4,64,1]{0,1,2:T(8,128)S(1)} %bitcast.40, f32[8,32,8,256]{3,2,1,0:T(8,128)} %bitcast.35), kind=kOutput, calls=%fused_computation.3 | convolution fusion | flops 25165824 | bytes 2229248 | tf_op jit(solution)/shard_map/dot_general | solution.py:67
  115.8 0.2 fusion.20
  116.0 0.3 fusion.6
  116.3 1.3 fusion.25
  117.6 2.3 %reshape.73 = f32[32,2,8192]{2,1,0:T(2,128)} reshape(f32[64,8192]{1,0:T(8,128)S(1)} %fusion.25) | data formatting | bytes 4194304 | tf_op jit(solution)/shard_map/reshape | solution.py:52
  119.9 4.0 %all-to-all-start.1 = ((f32[32,2,8192]{2,1,0:T(2,128)}), f32[32,2,8192]{2,1,0:T(2,128)S(1)}, u32[]{:S(2)}, u32[]{:S(2)}) async-start(f32[32,2,8192]{2,1,0:T(2,128)} %reshape.73), calls=%async_computation.1 | async-start | bytes 4194304 | tf_op jit(solution)/shard_map/all_to_all | solution.py:55
  123.9 0.7 copy.42
  124.6 48.2 %all-to-all-done.1 = f32[32,2,8192]{2,1,0:T(2,128)S(1)} async-done(((f32[32,2,8192]{2,1,0:T(2,128)}), f32[32,2,8192]{2,1,0:T(2,128)S(1)}, u32[]{:S(2)}, u32[]{:S(2)}) %all-to-all-start.1) | async-done | bytes 2097184 | tf_op jit(solution)/shard_map/all_to_all | solution.py:55
  172.8 2.5 %reshape.74 = f32[64,8192]{1,0:T(8,128)} reshape(f32[32,2,8192]{2,1,0:T(2,128)S(1)} %all-to-all-done.1) | data formatting | bytes 4194304 | tf_op jit(solution)/shard_map/reshape | solution.py:68
  175.3 2.7 %fusion = f32[4,32,256]{2,0,1:T(4,128)S(1)} fusion(f32[4,64,1]{0,1,2:T(8,128)S(1)} %bitcast.41, f32[8,32,8,256]{3,2,1,0:T(8,128)} %bitcast.34), kind=kOutput, calls=%fused_computation | convolution fusion | flops 25165824 | bytes 2229248 | tf_op jit(solution)/shard_map/dot_general | solution.py:67
  178.0 0.7 copy.43
  (28 shorter events, 1.8 us)
Async XLA Ops:
  0.6 1.6 copy-start
  0.6 47.6 %copy-start.1 = (f32[4,32,256]{2,1,0:T(8,128)S(1)}, f32[4,32,256]{2,1,0:T(8,128)}, u32[]{:S(2)}) copy-start(f32[4,32,256]{2,1,0:T(8,128)} %param.6) | copy-start | bytes 393220
  55.8 4.7 %copy-start.2 = (s32[128,16]{0,1:T(8,128)S(1)}, s32[128,16]{0,1:T(8,128)}, u32[]{:S(2)}) copy-start(s32[128,16]{0,1:T(8,128)} %param.8) | copy-start | bytes 24580
  55.8 6.8 %copy-start.3 = (s32[128,16]{0,1:T(8,128)S(1)}, s32[128,16]{0,1:T(8,128)}, u32[]{:S(2)}) copy-start(s32[128,16]{0,1:T(8,128)} %param.9) | copy-start | bytes 24580
  55.8 53.6 %all-to-all-start = ((f32[32,2,8192]{2,1,0:T(2,128)}), f32[32,2,8192]{2,1,0:T(2,128)}, u32[]{:S(2)}, u32[]{:S(2)}) async-start(f32[32,2,8192]{2,1,0:T(2,128)} %reshape.69), calls=%async_computation | async-start | bytes 4194304 | tf_op jit(solution)/shard_map/all_to_all | solution.py:55
  119.9 52.9 %all-to-all-start.1 = ((f32[32,2,8192]{2,1,0:T(2,128)}), f32[32,2,8192]{2,1,0:T(2,128)S(1)}, u32[]{:S(2)}, u32[]{:S(2)}) async-start(f32[32,2,8192]{2,1,0:T(2,128)} %reshape.73), calls=%async_computation.1 | async-start | bytes 4194304 | tf_op jit(solution)/shard_map/all_to_all | solution.py:55
where the time goes:
time: 179 us
  waiting for transfers between devices  94.6 us (53%)
  blocking collectives  42.3 us (24%)
  local copies, waits for them, and re-layouts  16.5 us (9%)
  matrix products  10.7 us (6%)
  starting transfers between devices  8.74 us (5%)
  other arithmetic  4.43 us (2%)
    all_to_all x2, waiting for transfers between devices, apply_galerkin(): lax.all_to_all(outgoing, 'mode', split_axis=0, concat_axis=0, tiled=True)  94.6 us
    psum x1, blocking collectives, local(): energy = lax.psum(jnp.sum(source_field * source_field), 'mode')  42.3 us
    all_to_all x2, starting transfers between devices, apply_galerkin(): lax.all_to_all(outgoing, 'mode', split_axis=0, concat_axis=0, tiled=True)  8.74 us
    reshape x2, local copies, waits for them, and re-layouts, apply_galerkin(): incoming.reshape(devices * slot_count, cell_count)  6.14 us
    reshape x2, local copies, waits for them, and re-layouts, apply_galerkin(): jnp.dot(packing, products, precision=highest)  5.76 us
    dot_general x2, matrix products, apply_galerkin(): jnp.dot(collect, incoming.reshape(devices * slot_count, cell_count), prec...  5.38 us
    dot_general x2, matrix products, apply_galerkin(): jnp.dot(packing, products, precision=highest)  3.89 us
  transfers between devices with their start and end apart: 2, of which 2 were waited for; matrix products, arithmetic and copies ran while one was open for 2% of the time, Pallas kernels for 0%

commit v1 on v0

--- a/solution.py
+++ b/solution.py
@@ -1,7 +1,15 @@
+import functools
+
 import jax
 import jax.numpy as jnp
 from jax import lax
+from jax.experimental import pallas as pl
+from jax.experimental.pallas import tpu as pltpu
 from jax.sharding import PartitionSpec as P
+
+LANES = 128
+SUB = 8
+MESH = pl.DeviceIdType.MESH
 
 
 def laplace(fields):
@@ -15,7 +23,7 @@
     )
 
 
-def local(source_field, coeff_fields, targets, dest_slot, coef_mode, coupling):
+def local_general(source_field, coeff_fields, targets, dest_slot, coef_mode, coupling):
     local_modes, grid_rows, grid_cols = source_field.shape
     cell_count = grid_rows * grid_cols
     devices = lax.axis_size("mode")
@@ -77,6 +85,293 @@
     return (first_image, second_image)
 
 
+def row_of(device):
+    core = device % 2
+    chip = device // 2
+    x = chip % 2
+    y = (chip // 2) % 2
+    z = chip // 4
+    place = y * 2 + (x + y) % 2
+    odd = z % 2
+    place = place + odd * (3 - 2 * place)
+    return (z * 4 + place) * 2 + core
+
+
+def device_of(row):
+    core = row % 2
+    step = row // 2
+    z = step // 4
+    place = step % 4
+    odd = z % 2
+    place = place + odd * (3 - 2 * place)
+    y = place // 2
+    x = (place + y) % 2
+    return ((z * 2 + y) * 2 + x) * 2 + core
+
+
+def split(values):
+    high = values.astype(jnp.bfloat16)
+    return high, (values - high.astype(jnp.float32)).astype(jnp.bfloat16)
+
+
+def side_sum(field):
+    cols = field.shape[1]
+    place = lax.broadcasted_iota(jnp.int32, field.shape, 1)
+    left = jnp.where(place == 0, 0.0, pltpu.roll(field, 1, 1))
+    right = jnp.where(place == cols - 1, 0.0, pltpu.roll(field, cols - 1, 1))
+    return left + right
+
+
+def end_sum(field):
+    rows = field.shape[0]
+    place = lax.broadcasted_iota(jnp.int32, field.shape, 0)
+    upper = jnp.where(place == 0, 0.0, pltpu.roll(field, 1, 0))
+    lower = jnp.where(place == rows - 1, 0.0, pltpu.roll(field, rows - 1, 0))
+    return upper + lower
+
+
+def kernel(
+    n, cell_total,
+    source, coeff, targets, dest, coef_mode, coupling,
+    first, second,
+    out_a, in_a, out_b, in_b, out_c, in_c, e_out, e_in, mine, above, below, a_high, a_low,
+    send_a, recv_a, send_b, recv_b, send_c, recv_c, send_e, recv_e, send_h, recv_h,
+):
+    modes_dev, rows, cols = source.shape
+    terms = coeff.shape[0]
+    modes, top = targets.shape
+    halves = cols // LANES
+    me = lax.axis_index("mode")
+    row = row_of(me)
+
+    barrier = pltpu.get_barrier_semaphore()
+
+    def greet(step, _):
+        pl.semaphore_signal(
+            barrier, inc=1, device_id={"mode": lax.rem(me + step, n)}, device_id_type=MESH
+        )
+        return 0
+
+    lax.fori_loop(1, n, greet, 0)
+
+    def tile(buf, index):
+        return buf.at[pl.ds(pl.multiple_of(index * SUB, SUB), SUB), :]
+
+    energy = jnp.zeros((1, LANES), jnp.float32)
+    for m in range(modes_dev):
+        field = source[m]
+        stencil = 4.0 * field - end_sum(field) - side_sum(field)
+        squares = jnp.sum(field * field, axis=0, keepdims=True)
+        for h in range(halves):
+            out_a[pl.ds(h * modes_dev + m, rows, stride=SUB), :] = stencil[:, h * LANES:(h + 1) * LANES]
+            energy = energy + squares[:, h * LANES:(h + 1) * LANES]
+    e_out[...] = energy
+
+    pl.semaphore_wait(barrier, n - 1)
+
+    def send_rows(step, _):
+        other = lax.rem(me + step, n)
+        pltpu.make_async_remote_copy(
+            src_ref=tile(out_a, row_of(other)), dst_ref=tile(in_a, me),
+            send_sem=send_a, recv_sem=recv_a,
+            device_id={"mode": other}, device_id_type=MESH,
+        ).start()
+        return 0
+
+    def send_energy(step, _):
+        other = lax.rem(me + step, n)
+        pltpu.make_async_remote_copy(
+            src_ref=e_out, dst_ref=e_in.at[me],
+            send_sem=send_e, recv_sem=recv_e,
+            device_id={"mode": other}, device_id_type=MESH,
+        ).start()
+        return 0
+
+    lax.fori_loop(1, n, send_rows, 0)
+    lax.fori_loop(1, n, send_energy, 0)
+    in_a[pl.ds(pl.multiple_of(me * SUB, SUB), SUB), :] = out_a[pl.ds(pl.multiple_of(row * SUB, SUB), SUB), :]
+    e_in[me] = energy
+
+    j_iota = lax.broadcasted_iota(jnp.int32, (modes, modes), 0)
+    p_iota = lax.broadcasted_iota(jnp.int32, (modes, modes), 1)
+    order = jnp.where((j_iota % modes_dev) * n + j_iota // modes_dev == p_iota, 1.0, 0.0)
+
+    def reordered(values):
+        return lax.dot_general(
+            values, order, (((0,), (0,)), ((), ())),
+            precision=lax.Precision.HIGHEST, preferred_element_type=jnp.float32,
+        )
+
+    place_t = reordered((dest[...] * n + targets[...]).astype(jnp.float32))
+    coef_t = reordered(coef_mode[...].astype(jnp.float32))
+    value_t = reordered(coupling[...])
+    k_iota = j_iota.astype(jnp.float32)
+    value = jnp.zeros((modes, modes), jnp.float32)
+    index = jnp.zeros((modes, modes), jnp.float32)
+    for t in range(top):
+        hit = place_t[t:t + 1, :] == k_iota
+        value = jnp.where(hit, value_t[t:t + 1, :], value)
+        index = jnp.where(hit, coef_t[t:t + 1, :], index)
+    for i in range(terms):
+        high, low = split(jnp.where(index == float(i), value, 0.0))
+        rows_i = pl.ds(i * modes, modes)
+        a_high[rows_i, :modes] = high
+        a_high[rows_i, modes:] = high
+        a_low[rows_i, :] = low
+
+    def galerkin(stencil):
+        high, low = split(stencil)
+        both = jnp.concatenate([high, low], axis=0)
+        total = jnp.zeros((modes, cols), jnp.float32)
+        for i in range(terms):
+            rows_i = pl.ds(i * modes, modes)
+            mixture = jnp.dot(a_high[rows_i, :], both, preferred_element_type=jnp.float32)
+            mixture = mixture + jnp.dot(a_low[rows_i, :], high, preferred_element_type=jnp.float32)
+            total = total + coeff[i, pl.ds(row, 1), :] * mixture
+        return total
+
+    def wait_all(out_buf, in_buf, send, recv):
+        count = pl.ds(0, (n - 1) * SUB)
+        pltpu.make_async_copy(out_buf.at[count, :], out_buf.at[count, :], send).wait()
+        pltpu.make_async_copy(in_buf.at[count, :], in_buf.at[count, :], recv).wait()
+
+    wait_all(out_a, in_a, send_a, recv_a)
+    stencil = jnp.concatenate(
+        [
+            jnp.concatenate(
+                [in_a[pl.ds(h * modes_dev + m, n, stride=SUB), :] for h in range(halves)], axis=1
+            )
+            for m in range(modes_dev)
+        ],
+        axis=0,
+    )
+    image = galerkin(stencil)
+    others = pl.ds(0, n - 1)
+    pltpu.make_async_copy(e_in.at[others], e_in.at[others], recv_e).wait()
+    pltpu.make_async_copy(e_in.at[others], e_in.at[others], send_e).wait()
+    whole = jnp.sum(jnp.sum(e_in[...], axis=0), axis=1, keepdims=True)
+    image = image / jnp.sqrt(whole / cell_total + 1e-06)
+    mine[...] = image
+
+    def halo(there, slot, sem):
+        return pltpu.make_async_remote_copy(
+            src_ref=mine, dst_ref=slot, send_sem=send_h.at[sem], recv_sem=recv_h.at[sem],
+            device_id={"mode": device_of(there)}, device_id_type=MESH,
+        )
+
+    @pl.when(row < rows - 1)
+    def _():
+        halo(row + 1, above, 0).start()
+
+    @pl.when(row > 0)
+    def _():
+        halo(row - 1, below, 1).start()
+
+    def place_tiles(buf, values):
+        for m in range(modes_dev):
+            for h in range(halves):
+                buf[pl.ds(h * modes_dev + m, n, stride=SUB), :] = values[
+                    m * n:(m + 1) * n, h * LANES:(h + 1) * LANES
+                ]
+
+    def send_back(out_buf, in_buf, send, recv):
+        def body(step, _):
+            other = lax.rem(me + step, n)
+            pltpu.make_async_remote_copy(
+                src_ref=tile(out_buf, other), dst_ref=tile(in_buf, row),
+                send_sem=send, recv_sem=recv,
+                device_id={"mode": other}, device_id_type=MESH,
+            ).start()
+            return 0
+
+        lax.fori_loop(1, n, body, 0)
+        in_buf[pl.ds(pl.multiple_of(row * SUB, SUB), SUB), :] = out_buf[
+            pl.ds(pl.multiple_of(me * SUB, SUB), SUB), :
+        ]
+
+    def take_tiles(buf, result):
+        for m in range(modes_dev):
+            for h in range(halves):
+                result[m, :, h * LANES:(h + 1) * LANES] = buf[pl.ds(h * modes_dev + m, rows, stride=SUB), :]
+
+    place_tiles(out_b, image)
+    send_back(out_b, in_b, send_b, recv_b)
+
+    inner = 4.0 * image - side_sum(image)
+
+    @pl.when(row == 0)
+    def _():
+        above[...] = jnp.zeros_like(above)
+
+    @pl.when(row == rows - 1)
+    def _():
+        below[...] = jnp.zeros_like(below)
+
+    @pl.when(row > 0)
+    def _():
+        halo(row - 1, above, 0).wait_recv()
+
+    @pl.when(row < rows - 1)
+    def _():
+        halo(row + 1, below, 1).wait_recv()
+
+    image = galerkin(inner - above[...] - below[...])
+    place_tiles(out_c, image)
+    send_back(out_c, in_c, send_c, recv_c)
+
+    wait_all(out_b, in_b, send_b, recv_b)
+    take_tiles(in_b, first)
+
+    @pl.when(row < rows - 1)
+    def _():
+        halo(row + 1, above, 0).wait_send()
+
+    @pl.when(row > 0)
+    def _():
+        halo(row - 1, below, 1).wait_send()
+
+    wait_all(out_c, in_c, send_c, recv_c)
+    take_tiles(in_c, second)
+
+
+def local_rows(source_field, coeff_fields, targets, dest_slot, coef_mode, coupling):
+    modes_dev, rows, cols = source_field.shape
+    n = lax.axis_size("mode")
+    modes = targets.shape[0]
+    terms = coeff_fields.shape[0]
+    tiles = pltpu.VMEM((n * SUB, LANES), jnp.float32)
+    grid_row = pltpu.VMEM((modes, cols), jnp.float32)
+    image = jax.ShapeDtypeStruct(source_field.shape, jnp.float32)
+    in_vmem = pl.BlockSpec(memory_space=pltpu.VMEM)
+    dma = pltpu.SemaphoreType.DMA
+    return pl.pallas_call(
+        functools.partial(kernel, n, float(modes * rows * cols)),
+        out_shape=(image, image),
+        in_specs=[in_vmem] * 6,
+        out_specs=(in_vmem, in_vmem),
+        scratch_shapes=[tiles] * 6
+        + [
+            pltpu.VMEM((1, LANES), jnp.float32),
+            pltpu.VMEM((n, 1, LANES), jnp.float32),
+            grid_row, grid_row, grid_row,
+            pltpu.VMEM((terms * modes, 2 * modes), jnp.bfloat16),
+            pltpu.VMEM((terms * modes, modes), jnp.bfloat16),
+        ]
+        + [dma] * 8 + [dma((2,)), dma((2,))],
+        compiler_params=pltpu.CompilerParams(
+            collective_id=0, has_side_effects=True, vmem_limit_bytes=32 * 1024 * 1024
+        ),
+    )(source_field, coeff_fields, targets, dest_slot, coef_mode, coupling)
+
+
+def local(source_field, *rest):
+    modes_dev, rows, cols = source_field.shape
+    n = lax.axis_size("mode")
+    if n == rows and n % SUB == 0 and cols % LANES == 0 and modes_dev * (cols // LANES) == SUB:
+        return local_rows(source_field, *rest)
+    return local_general(source_field, *rest)
+
+
 def solution(mesh):
     in_specs = (P(("group", "mode"), None, None), P("group", None, None), P(), P(), P(), P())
     out_specs = (P(("group", "mode"), None, None), P(("group", "mode"), None, None))

time: 179 us -> 28.2 us (0.16)
  waiting for transfers between devices: 94.6 us -> 0 us
  blocking collectives: 42.3 us -> 0 us
  Pallas kernels: 0 us -> 22.5 us
  local copies, waits for them, and re-layouts: 16.5 us -> 4.62 us
  matrix products: 10.7 us -> 0 us
  starting transfers between devices: 8.74 us -> 0 us
  other arithmetic: 4.43 us -> 0 us
    all_to_all x2 -> x0, waiting for transfers between devices: 94.6 us -> none  [apply_galerkin(): lax.all_to_all(outgoing, 'mode', split_axis=0, concat_axis=0, tiled=True)]
    psum x1 -> x0, blocking collectives: 42.3 us -> none  [local(): energy = lax.psum(jnp.sum(source_field * source_field), 'mode')]
    pallas_call x0 -> x1, Pallas kernels: none -> 22.5 us  [local_rows(): pl.pallas_call(functools.partial(kernel, n, float(modes * rows * cols)),...]
    reshape x5 -> x0, local copies, waits for them, and re-layouts: 12 us -> none  [the longest x2 6.14 us: apply_galerkin(): incoming.reshape(devices * slot_count, cell_count)]
    dot_general x6 -> x0, matrix products: 10.7 us -> none  [the longest x2 5.38 us: apply_galerkin(): jnp.dot(collect, incoming.reshape(devices * slot_count, cell_count), prec...]
    all_to_all x2 -> x0, starting transfers between devices: 8.74 us -> none  [apply_galerkin(): lax.all_to_all(outgoing, 'mode', split_axis=0, concat_axis=0, tiled=True)]
    another operation x2 -> x0, other arithmetic: 1.82 us -> none  [the longest x1 1.72 us: apply_galerkin(): jnp.cumsum(all_hot, axis=1) - all_hot]
    unnamed x14 -> x16, local copies, waits for them, and re-layouts: 2.92 us -> 4.62 us
  transfers between devices with their start and end apart: 2 -> 0, of which waited for: 2 -> 0; matrix products, arithmetic and copies ran while one was open for 2% -> 0% of each run, Pallas kernels for 0% -> 0%
where the time goes in v1:
time: 28.2 us; the launch traced here: 27.8 us
  Pallas kernels  22.5 us (80%)
  local copies, waits for them, and re-layouts  4.62 us (16%)
  between operations  0.68 us (2%)
    pallas_call x1, Pallas kernels, local_rows(): pl.pallas_call(functools.partial(kernel, n, float(modes * rows * cols)),...  22.5 us
    unnamed x16, local copies, waits for them, and re-layouts  4.62 us

profile of v1, /device:TPU:0, one launch (start us, length us, event | category | flops | bytes accessed | tf_op | source)
XLA Modules:
  0.0 27.8 jit_solution(7553582957132810861)
XLA Ops:
  0.6 0.0 copy-start.2
  0.6 0.0 copy-start.1
  0.6 0.8 %copy.8.targets = s32[128,16]{1,0:T(8,128)S(1)} copy(s32[128,16]{0,1:T(8,128)} %param.8) | data formatting | bytes 16384 | tf_op args[2]
  1.5 0.0 copy-done.2
  1.5 0.0 copy-start.3
  1.5 0.1 copy.9.dest
  1.6 0.6 %copy-done.3 = s32[128,16]{0,1:T(8,128)S(1)} copy-done((s32[128,16]{0,1:T(8,128)S(1)}, s32[128,16]{0,1:T(8,128)}, u32[]{:S(2)}) %copy-start.3) | copy-done | bytes 8216
  2.2 0.0 copy-start.4
  2.2 0.1 copy.10.coef_mode
  2.3 0.6 %copy-done.4 = f32[128,16]{0,1:T(8,128)S(1)} copy-done((f32[128,16]{0,1:T(8,128)S(1)}, f32[128,16]{0,1:T(8,128)}, u32[]{:S(2)}) %copy-start.4) | copy-done | bytes 8216
  2.9 0.1 copy.11.coupling
  3.0 0.0 copy-done.1
  3.0 0.0 copy-start
  3.0 1.0 %copy-done = f32[11,32,256]{2,1,0:T(8,128)S(1)} copy-done((f32[11,32,256]{2,1,0:T(8,128)S(1)}, f32[11,32,256]{2,1,0:T(8,128)}, u32[]{:S(2)}) %copy-start) | copy-done | bytes 360472
  4.0 22.5 %shard_map.77 = (f32[4,32,256]{2,1,0:T(8,128)S(1)}, f32[4,32,256]{2,1,0:T(8,128)S(1)}) custom-call(f32[4,32,256]{2,1,0:T(8,128)S(1)} %copy-done.1, f32[11,32,256]{2,1,0:T(8,128)S(1)} %copy-done, s32[128,16]{1,0:T(8,128)S(1)} %copy.8.targets, s32[128,16]{1,0:T(8,128)S(1)} %copy.9.dest, s32[128,16]{1,0:T(8,128)S(1)} %copy.10.coef_mode, ...), custom_call_target="tpu_custom_call" | custom-call | tf_op jit(solution)/shard_map/pallas_call | solution.py:347
  26.5 0.7 %copy.14 = f32[4,32,256]{2,1,0:T(8,128)} copy(f32[4,32,256]{2,1,0:T(8,128)S(1)} %get-tuple-element.4) | data formatting | bytes 262144
  27.2 0.7 %copy.15 = f32[4,32,256]{2,1,0:T(8,128)} copy(f32[4,32,256]{2,1,0:T(8,128)S(1)} %get-tuple-element.5) | data formatting | bytes 262144
Async XLA Ops:
  0.6 0.9 %copy-start.2 = (s32[128,16]{0,1:T(8,128)S(1)}, s32[128,16]{0,1:T(8,128)}, u32[]{:S(2)}) copy-start(s32[128,16]{0,1:T(8,128)} %param.9) | copy-start | bytes 24580
  0.6 2.3 %copy-start.1 = (f32[4,32,256]{2,1,0:T(8,128)S(1)}, f32[4,32,256]{2,1,0:T(8,128)}, u32[]{:S(2)}) copy-start(f32[4,32,256]{2,1,0:T(8,128)} %source.1) | copy-start | bytes 393220
  1.5 0.7 %copy-start.3 = (s32[128,16]{0,1:T(8,128)S(1)}, s32[128,16]{0,1:T(8,128)}, u32[]{:S(2)}) copy-start(s32[128,16]{0,1:T(8,128)} %param.10) | copy-start | bytes 24580
  2.2 0.7 %copy-start.4 = (f32[128,16]{0,1:T(8,128)S(1)}, f32[128,16]{0,1:T(8,128)}, u32[]{:S(2)}) copy-start(f32[128,16]{0,1:T(8,128)} %param.11) | copy-start | bytes 24580
  3.0 1.0 %copy-start = (f32[11,32,256]{2,1,0:T(8,128)S(1)}, f32[11,32,256]{2,1,0:T(8,128)}, u32[]{:S(2)}) copy-start(f32[11,32,256]{2,1,0:T(8,128)} %coeff.1) | copy-start | bytes 1081348

commit v2 on v1

--- a/solution.py
+++ b/solution.py
@@ -132,17 +132,28 @@
 
 def kernel(
     n, cell_total,
+    source_hbm, coeff_hbm, targets_hbm, dest_hbm, coef_mode_hbm, coupling_hbm,
+    first, second,
     source, coeff, targets, dest, coef_mode, coupling,
-    first, second,
     out_a, in_a, out_b, in_b, out_c, in_c, e_out, e_in, mine, above, below, a_high, a_low,
-    send_a, recv_a, send_b, recv_b, send_c, recv_c, send_e, recv_e, send_h, recv_h,
+    send_a, recv_a, send_b, recv_b, send_c, recv_c, send_e, recv_e, send_h, recv_h, load_source, load_rest,
 ):
     modes_dev, rows, cols = source.shape
     terms = coeff.shape[0]
-    modes, top = targets.shape
+    top, modes = targets.shape
     halves = cols // LANES
     me = lax.axis_index("mode")
     row = row_of(me)
+    block = pl.multiple_of(row // SUB * SUB, SUB)
+
+    loads = [pltpu.make_async_copy(source_hbm, source, load_source)]
+    pairs = (
+        (targets_hbm, targets), (dest_hbm, dest), (coef_mode_hbm, coef_mode), (coupling_hbm, coupling),
+        (coeff_hbm.at[:, pl.ds(block, SUB), :], coeff),
+    )
+    loads += [pltpu.make_async_copy(src, dst, load_rest.at[k]) for k, (src, dst) in enumerate(pairs)]
+    for load in loads:
+        load.start()
 
     barrier = pltpu.get_barrier_semaphore()
 
@@ -157,6 +168,7 @@
     def tile(buf, index):
         return buf.at[pl.ds(pl.multiple_of(index * SUB, SUB), SUB), :]
 
+    loads[0].wait()
     energy = jnp.zeros((1, LANES), jnp.float32)
     for m in range(modes_dev):
         field = source[m]
@@ -188,17 +200,18 @@
         return 0
 
     lax.fori_loop(1, n, send_rows, 0)
-    lax.fori_loop(1, n, send_energy, 0)
+    e_in[me] = energy
     in_a[pl.ds(pl.multiple_of(me * SUB, SUB), SUB), :] = out_a[pl.ds(pl.multiple_of(row * SUB, SUB), SUB), :]
-    e_in[me] = energy
-
+
+    for load in loads[1:]:
+        load.wait()
     j_iota = lax.broadcasted_iota(jnp.int32, (modes, modes), 0)
     p_iota = lax.broadcasted_iota(jnp.int32, (modes, modes), 1)
     order = jnp.where((j_iota % modes_dev) * n + j_iota // modes_dev == p_iota, 1.0, 0.0)
 
     def reordered(values):
         return lax.dot_general(
-            values, order, (((0,), (0,)), ((), ())),
+            values, order, (((1,), (0,)), ((), ())),
             precision=lax.Precision.HIGHEST, preferred_element_type=jnp.float32,
         )
 
@@ -227,7 +240,7 @@
             rows_i = pl.ds(i * modes, modes)
             mixture = jnp.dot(a_high[rows_i, :], both, preferred_element_type=jnp.float32)
             mixture = mixture + jnp.dot(a_low[rows_i, :], high, preferred_element_type=jnp.float32)
-            total = total + coeff[i, pl.ds(row, 1), :] * mixture
+            total = total + coeff[i, pl.ds(row - block, 1), :] * mixture
         return total
 
     def wait_all(out_buf, in_buf, send, recv):
@@ -246,11 +259,6 @@
         axis=0,
     )
     image = galerkin(stencil)
-    others = pl.ds(0, n - 1)
-    pltpu.make_async_copy(e_in.at[others], e_in.at[others], recv_e).wait()
-    pltpu.make_async_copy(e_in.at[others], e_in.at[others], send_e).wait()
-    whole = jnp.sum(jnp.sum(e_in[...], axis=0), axis=1, keepdims=True)
-    image = image / jnp.sqrt(whole / cell_total + 1e-06)
     mine[...] = image
 
     def halo(there, slot, sem):
@@ -292,11 +300,14 @@
     def take_tiles(buf, result):
         for m in range(modes_dev):
             for h in range(halves):
-                result[m, :, h * LANES:(h + 1) * LANES] = buf[pl.ds(h * modes_dev + m, rows, stride=SUB), :]
+                result[m, :, h * LANES:(h + 1) * LANES] = buf[
+                    pl.ds(h * modes_dev + m, rows, stride=SUB), :
+                ] * scale
 
     place_tiles(out_b, image)
     send_back(out_b, in_b, send_b, recv_b)
 
+    lax.fori_loop(1, n, send_energy, 0)
     inner = 4.0 * image - side_sum(image)
 
     @pl.when(row == 0)
@@ -320,6 +331,11 @@
     send_back(out_c, in_c, send_c, recv_c)
 
     wait_all(out_b, in_b, send_b, recv_b)
+    others = pl.ds(0, n - 1)
+    pltpu.make_async_copy(e_in.at[others], e_in.at[others], recv_e).wait()
+    pltpu.make_async_copy(e_in.at[others], e_in.at[others], send_e).wait()
+    whole = jnp.sum(jnp.sum(e_in[...], axis=0), axis=1, keepdims=True)
+    scale = 1.0 / jnp.sqrt(whole / cell_total + 1e-06)
     take_tiles(in_b, first)
 
     @pl.when(row < rows - 1)
@@ -343,13 +359,21 @@
     grid_row = pltpu.VMEM((modes, cols), jnp.float32)
     image = jax.ShapeDtypeStruct(source_field.shape, jnp.float32)
     in_vmem = pl.BlockSpec(memory_space=pltpu.VMEM)
+    in_hbm = pl.BlockSpec(memory_space=pltpu.HBM)
+    table = (targets.shape[1], modes)
     dma = pltpu.SemaphoreType.DMA
     return pl.pallas_call(
         functools.partial(kernel, n, float(modes * rows * cols)),
         out_shape=(image, image),
-        in_specs=[in_vmem] * 6,
+        in_specs=[in_hbm] * 6,
         out_specs=(in_vmem, in_vmem),
-        scratch_shapes=[tiles] * 6
+        scratch_shapes=[
+            pltpu.VMEM(source_field.shape, jnp.float32),
+            pltpu.VMEM((terms, SUB, cols), jnp.float32),
+            pltpu.VMEM(table, jnp.int32), pltpu.VMEM(table, jnp.int32),
+            pltpu.VMEM(table, jnp.int32), pltpu.VMEM(table, jnp.float32),
+        ]
+        + [tiles] * 6
         + [
             pltpu.VMEM((1, LANES), jnp.float32),
             pltpu.VMEM((n, 1, LANES), jnp.float32),
@@ -357,17 +381,17 @@
             pltpu.VMEM((terms * modes, 2 * modes), jnp.bfloat16),
             pltpu.VMEM((terms * modes, modes), jnp.bfloat16),
         ]
-        + [dma] * 8 + [dma((2,)), dma((2,))],
+        + [dma] * 8 + [dma((2,)), dma((2,)), dma, dma((5,))],
         compiler_params=pltpu.CompilerParams(
-            collective_id=0, has_side_effects=True, vmem_limit_bytes=32 * 1024 * 1024
+            collective_id=0, has_side_effects=True, vmem_limit_bytes=60 * 1024 * 1024
         ),
-    )(source_field, coeff_fields, targets, dest_slot, coef_mode, coupling)
+    )(source_field, coeff_fields, targets.T, dest_slot.T, coef_mode.T, coupling.T)
 
 
 def local(source_field, *rest):
     modes_dev, rows, cols = source_field.shape
     n = lax.axis_size("mode")
-    if n == rows and n % SUB == 0 and cols % LANES == 0 and modes_dev * (cols // LANES) == SUB:
+    if n == rows and n >= 16 and n & (n - 1) == 0 and cols % LANES == 0 and modes_dev * (cols // LANES) == SUB:
         return local_rows(source_field, *rest)
     return local_general(source_field, *rest)
 

time: 28.2 us -> 26.2 us (0.929)
  local copies, waits for them, and re-layouts: 4.62 us -> 2.26 us
  Pallas kernels: 22.5 us -> 23.1 us
    unnamed x16 -> x4, local copies, waits for them, and re-layouts: 4.62 us -> 2.26 us
    pallas_call x1, Pallas kernels: 22.5 us -> 23.1 us  [local_rows(): pl.pallas_call(functools.partial(kernel, n, float(modes * rows * cols)),...]
where the time goes in v2:
time: 26.2 us; the launch traced here: 26 us
  Pallas kernels  23.1 us (88%)
  local copies, waits for them, and re-layouts  2.26 us (9%)
  between operations  0.65 us (2%)
    pallas_call x1, Pallas kernels, local_rows(): pl.pallas_call(functools.partial(kernel, n, float(modes * rows * cols)),...  23.1 us
    unnamed x4, local copies, waits for them, and re-layouts  2.26 us

profile of v2, /device:TPU:0, one launch (start us, length us, event | category | flops | bytes accessed | tf_op | source)
XLA Modules:
  0.0 26.0 jit_solution(13809009550822582761)
XLA Ops:
  0.6 23.1 %shard_map.77 = (f32[4,32,256]{2,1,0:T(8,128)}, f32[4,32,256]{2,1,0:T(8,128)}) custom-call(f32[4,32,256]{2,1,0:T(8,128)} %source_hbm.1, f32[11,32,256]{2,1,0:T(8,128)} %coeff_hbm.1, s32[16,128]{1,0:T(8,128)} %bitcast.4, s32[16,128]{1,0:T(8,128)} %bitcast.5, s32[16,128]{1,0:T(8,128)} %bitcast.6, f32[16,128]{1,0:T(8,128)} %bitcast.7), custom_call_target="tpu_custom_call" | custom-call | tf_op jit(solution)/shard_map/pallas_call | solution.py:365
  23.8 0.0 copy-start
  23.8 1.6 %copy.10 = f32[4,32,256]{2,1,0:T(8,128)} copy(f32[4,32,256]{2,1,0:T(8,128)} %get-tuple-element.4) | data formatting | bytes 262144
  25.4 0.0 copy-done
  25.4 0.7 %copy.11 = f32[4,32,256]{2,1,0:T(8,128)} copy(f32[4,32,256]{2,1,0:T(8,128)S(1)} %copy-done) | data formatting | bytes 262144
Async XLA Ops:
  23.8 1.6 %copy-start = (f32[4,32,256]{2,1,0:T(8,128)S(1)}, f32[4,32,256]{2,1,0:T(8,128)}, u32[]{:S(2)}) copy-start(f32[4,32,256]{2,1,0:T(8,128)} %get-tuple-element.5) | copy-start | bytes 393220

commit v3 on v2

--- a/solution.py
+++ b/solution.py
@@ -383,9 +383,12 @@
         ]
         + [dma] * 8 + [dma((2,)), dma((2,)), dma, dma((5,))],
         compiler_params=pltpu.CompilerParams(
-            collective_id=0, has_side_effects=True, vmem_limit_bytes=60 * 1024 * 1024
+            collective_id=0, has_side_effects=True, vmem_limit_bytes=32 * 1024 * 1024
         ),
-    )(source_field, coeff_fields, targets.T, dest_slot.T, coef_mode.T, coupling.T)
+    )(*[
+        pltpu.with_memory_space_constraint(value, pltpu.HBM)
+        for value in (source_field, coeff_fields, targets.T, dest_slot.T, coef_mode.T, coupling.T)
+    ])
 
 
 def local(source_field, *rest):

time: 26.2 us -> 24.6 us (0.939)
  local copies, waits for them, and re-layouts: 2.26 us -> 1.31 us
  Pallas kernels: 23.1 us -> 22.5 us
    unnamed x4 -> x2, local copies, waits for them, and re-layouts: 2.26 us -> 1.31 us
    pallas_call x1, Pallas kernels: 23.1 us -> 22.5 us  [local_rows(): pl.pallas_call(functools.partial(kernel, n, float(modes * rows * cols)),...]
where the time goes in v3:
time: 24.6 us; the launch traced here: 24.4 us
  Pallas kernels  22.5 us (91%)
  local copies, waits for them, and re-layouts  1.31 us (5%)
  between operations  0.64 us (3%)
    pallas_call x1, Pallas kernels, local_rows(): pl.pallas_call(functools.partial(kernel, n, float(modes * rows * cols)),...  22.5 us
    unnamed x2, local copies, waits for them, and re-layouts  1.31 us

profile of v3, /device:TPU:0, one launch (start us, length us, event | category | flops | bytes accessed | tf_op | source)
XLA Modules:
  0.0 24.4 jit_solution(2980350699197685974)
XLA Ops:
  0.6 22.5 %shard_map.77 = (f32[4,32,256]{2,1,0:T(8,128)S(1)}, f32[4,32,256]{2,1,0:T(8,128)S(1)}) custom-call(f32[4,32,256]{2,1,0:T(8,128)} %source_hbm.1, f32[11,32,256]{2,1,0:T(8,128)} %coeff_hbm.1, s32[16,128]{1,0:T(8,128)} %bitcast.4, s32[16,128]{1,0:T(8,128)} %bitcast.5, s32[16,128]{1,0:T(8,128)} %bitcast.6, f32[16,128]{1,0:T(8,128)} %bitcast.7), custom_call_target="tpu_custom_call" | custom-call | tf_op jit(solution)/shard_map/pallas_call | solution.py:365
  23.1 0.7 %copy.10 = f32[4,32,256]{2,1,0:T(8,128)} copy(f32[4,32,256]{2,1,0:T(8,128)S(1)} %get-tuple-element.4) | data formatting | bytes 262144
  23.8 0.7 %copy.11 = f32[4,32,256]{2,1,0:T(8,128)} copy(f32[4,32,256]{2,1,0:T(8,128)S(1)} %get-tuple-element.5) | data formatting | bytes 262144

commit v4 on v3

--- a/solution.py
+++ b/solution.py
@@ -243,12 +243,11 @@
             total = total + coeff[i, pl.ds(row - block, 1), :] * mixture
         return total
 
-    def wait_all(out_buf, in_buf, send, recv):
+    def wait_bytes(buf, sem):
         count = pl.ds(0, (n - 1) * SUB)
-        pltpu.make_async_copy(out_buf.at[count, :], out_buf.at[count, :], send).wait()
-        pltpu.make_async_copy(in_buf.at[count, :], in_buf.at[count, :], recv).wait()
-
-    wait_all(out_a, in_a, send_a, recv_a)
+        pltpu.make_async_copy(buf.at[count, :], buf.at[count, :], sem).wait()
+
+    wait_bytes(in_a, recv_a)
     stencil = jnp.concatenate(
         [
             jnp.concatenate(
@@ -330,7 +329,7 @@
     place_tiles(out_c, image)
     send_back(out_c, in_c, send_c, recv_c)
 
-    wait_all(out_b, in_b, send_b, recv_b)
+    wait_bytes(in_b, recv_b)
     others = pl.ds(0, n - 1)
     pltpu.make_async_copy(e_in.at[others], e_in.at[others], recv_e).wait()
     pltpu.make_async_copy(e_in.at[others], e_in.at[others], send_e).wait()
@@ -346,8 +345,10 @@
     def _():
         halo(row - 1, below, 1).wait_send()
 
-    wait_all(out_c, in_c, send_c, recv_c)
+    wait_bytes(in_c, recv_c)
     take_tiles(in_c, second)
+    for buf, sem in ((out_a, send_a), (out_b, send_b), (out_c, send_c)):
+        wait_bytes(buf, sem)
 
 
 def local_rows(source_field, coeff_fields, targets, dest_slot, coef_mode, coupling):

time: 24.6 us -> 24.6 us (level)
  no operation moved by 1% of the time
where the time goes in v4:
time: 24.6 us; the launch traced here: 24.4 us
  Pallas kernels  22.5 us (91%)
  local copies, waits for them, and re-layouts  1.31 us (5%)
  between operations  0.64 us (3%)
    pallas_call x1, Pallas kernels, local_rows(): pl.pallas_call(functools.partial(kernel, n, float(modes * rows * cols)),...  22.5 us
    unnamed x2, local copies, waits for them, and re-layouts  1.31 us

profile of v4, /device:TPU:0, one launch (start us, length us, event | category | flops | bytes accessed | tf_op | source)
XLA Modules:
  0.0 24.4 jit_solution(2894200295108302574)
XLA Ops:
  0.6 22.5 %shard_map.77 = (f32[4,32,256]{2,1,0:T(8,128)S(1)}, f32[4,32,256]{2,1,0:T(8,128)S(1)}) custom-call(f32[4,32,256]{2,1,0:T(8,128)} %source_hbm.1, f32[11,32,256]{2,1,0:T(8,128)} %coeff_hbm.1, s32[16,128]{1,0:T(8,128)} %bitcast.4, s32[16,128]{1,0:T(8,128)} %bitcast.5, s32[16,128]{1,0:T(8,128)} %bitcast.6, f32[16,128]{1,0:T(8,128)} %bitcast.7), custom_call_target="tpu_custom_call" | custom-call | tf_op jit(solution)/shard_map/pallas_call | solution.py:366
  23.1 0.7 %copy.10 = f32[4,32,256]{2,1,0:T(8,128)} copy(f32[4,32,256]{2,1,0:T(8,128)S(1)} %get-tuple-element.4) | data formatting | bytes 262144
  23.8 0.7 %copy.11 = f32[4,32,256]{2,1,0:T(8,128)} copy(f32[4,32,256]{2,1,0:T(8,128)S(1)} %get-tuple-element.5) | data formatting | bytes 262144
